TPU v7x, 128 devices: a whole 4x4x4 slice. The times are simulated.
128 devices in a mesh: dp: 4 (over z), ctx: 32 (over x, y, core).
Axes of the slice: x: 4, y: 4, z: 4, core: 2. Of those that a mesh axis runs over, the one named last changes fastest.
Arguments:
- queries: bfloat16 [4, 4096, 4096], P('dp', 'ctx'), may hold values from -2.5 to 2.5
- key_state_vectors: bfloat16 [4, 4096, 512], P('dp', 'ctx'), may hold values from -2.5 to 2.5
- value_state_vectors: bfloat16 [4, 4096, 512], P('dp', 'ctx'), may hold values from -4 to 4
- output_gradient: bfloat16 [4, 4096, 4096], P('dp', 'ctx'), may hold values from -6 to 6
- lengths: int32 [4, 16], replicated, may hold values from 1 to 768, 4096 in all within a row
Outputs:
- grad_queries: bfloat16 [4, 4096, 4096], P('dp', 'ctx')
- grad_keys: bfloat16 [4, 4096, 512], P('dp', 'ctx')
- grad_values: bfloat16 [4, 4096, 512], P('dp', 'ctx')
Inputs may be any that keep to these rules, and one draw needn't show every extreme that they name: Each row holds 16 document lengths that sum to 4096; the longest in each row is exactly 768.
All inputs are finite; a program needn't handle non-finite values.
Results may differ from a plain program's by a relative error of at most 0.0055.
Values may be sent and summed in bfloat16 or wider, within the bound.
A program may use at most 128 MiB of HBM per device.

v0:
```python
import math

import jax
import jax.numpy as jnp
from jax import lax
from jax.experimental import pallas as pl
from jax.experimental.pallas import tpu as pltpu
from jax.sharding import PartitionSpec as P

HEAD = 128
ROWS = 128
PAIR = 2 * ROWS
GROUP = 8
GROUPS = 2
SIDE = 4
DOCS = 16
SLOTS = 4
FACTOR = 1.0 / math.sqrt(HEAD)
LOG2_FACTOR = FACTOR * math.log2(math.e)
BF16 = jnp.bfloat16
F32 = jnp.float32
NT = (((1,), (1,)), ((), ()))
NN = (((1,), (0,)), ((), ()))


def dot(a, b, dims):
    return lax.dot_general(a, b, dims, preferred_element_type=F32)


def kernel(
    lengths, q_hbm, k_hbm, v_hbm, g_hbm,
    dq_hbm, dk_hbm, dv_hbm,
    q_s, g_s, kv, relay, bias, w_s, dp_s, l_s, d_s, p_s, ds_s, own, out_stage, ret_send, ret, fwd_stage, back,
    dq_s, kt_s,
    q_sem, kv_sem, kv_lsem, y_send, y_recv, x_send, x_recv,
    r_send, r_recv, b_send, b_recv, o_sem, o_send, o_recv, dq_sem, dq_send, dq_recv,
):
    dp_at = lax.axis_index("dp")
    me = lax.axis_index("ctx")
    chip, core = me // 2, me % 2
    px, py = chip // SIDE, chip % SIDE
    other = 1 - core

    def at(x, y, k):
        return {"ctx": (((x + SIDE) % SIDE) * SIDE + (y + SIDE) % SIDE) * 2 + k}

    sibling = at(px, py, other)
    x_next, x_prev = at(px + 1, py, core), at(px - 1, py, core)
    ring = [None] + [at(px, py + j, core) for j in range(1, SIDE)]

    def remote(src, dst, send, recv, where):
        return pltpu.make_async_remote_copy(
            src_ref=src, dst_ref=dst, send_sem=send, recv_sem=recv,
            device_id=where, device_id_type=pl.DeviceIdType.MESH,
        )

    mine = pl.ds(pl.multiple_of(core * ROWS, ROWS), ROWS)
    theirs = pl.ds(pl.multiple_of(other * ROWS, ROWS), ROWS)
    half = GROUPS * GROUP * HEAD
    my_heads = pl.ds(pl.multiple_of(core * half, HEAD), half)
    their_heads = pl.ds(pl.multiple_of(other * half, HEAD), half)

    def group_cols(k, gi):
        return pl.ds(pl.multiple_of((k * GROUPS + gi) * HEAD, HEAD), HEAD)

    local = []
    for gi in range(GROUPS):
        for t, src in enumerate((k_hbm, v_hbm)):
            cp = pltpu.make_async_copy(src.at[:, group_cols(core, gi)], kv.at[gi, 0, t, mine], kv_lsem.at[gi, t])
            cp.start()
            local.append(cp)
    q_local = []
    for t, (src, dst) in enumerate(((q_hbm, q_s), (g_hbm, g_s))):
        cp = pltpu.make_async_copy(src.at[:, my_heads], dst.at[mine], q_sem.at[2, t])
        cp.start()
        q_local.append(cp)

    barrier = pltpu.get_barrier_semaphore()
    for peer in [sibling, x_next, x_prev] + ring[1:]:
        pl.semaphore_signal(barrier, inc=1, device_id=peer, device_id_type=pl.DeviceIdType.MESH)
    pl.semaphore_wait(barrier, 6)

    kv_swap = []
    for gi in range(GROUPS):
        for t, src in enumerate((k_hbm, v_hbm)):
            cp = remote(
                src.at[:, group_cols(other, gi)], kv.at[gi, 0, t, mine], kv_sem.at[0, gi, t], kv_sem.at[1, gi, t], sibling
            )
            cp.start()
            kv_swap.append(cp)
    q_swap = []
    for t, (src, dst) in enumerate(((q_hbm, q_s), (g_hbm, g_s))):
        cp = remote(src.at[:, their_heads], dst.at[mine], q_sem.at[0, t], q_sem.at[1, t], sibling)
        cp.start()
        q_swap.append(cp)

    def x_copy(gi):
        return remote(kv.at[gi, 0], relay.at[gi], x_send.at[gi], x_recv.at[gi], x_next)

    def y_copy(gi, j, src):
        return remote(src, kv.at[gi, j], y_send.at[gi, j], y_recv.at[gi, j], ring[j])

    for gi in range(GROUPS):
        for t in range(2):
            local[2 * gi + t].wait()
            kv_swap[2 * gi + t].wait_recv()

        @pl.when(py > 0)
        def _():
            x_copy(gi).start()

        for j in range(1, SLOTS):

            @pl.when(py + j < SIDE)
            def _():
                y_copy(gi, j, kv.at[gi, 0]).start()

    q_pos = chip * PAIR + lax.broadcasted_iota(jnp.int32, (8, PAIR), 1)
    start = jnp.zeros((8, PAIR), jnp.int32)
    bound = jnp.int32(0)
    for d in range(DOCS):
        bound = bound + lengths[dp_at, d]
        start = jnp.where(bound <= q_pos, jnp.maximum(start, bound), start)
    start, q_pos = start[:1], q_pos[:1]
    for j in range(SLOTS):
        k_pos = (chip - j) * PAIR + lax.broadcasted_iota(jnp.int32, (PAIR, PAIR), 0)
        bias[j] = jnp.where((k_pos >= start) & (k_pos <= q_pos), 0.0, -1e30)

    for gi in range(GROUPS):

        @pl.when(py > 0)
        def _():
            x_copy(gi).wait_recv()

        for j in range(1, SLOTS):

            @pl.when(py + j >= SIDE)
            def _():
                y_copy(gi, j, relay.at[gi]).start()

    for t in range(2):
        q_local[t].wait()
        q_swap[t].wait_recv()

    def head_cols(gi, e):
        return pl.ds(pl.multiple_of((gi * GROUP + e) * HEAD, HEAD), HEAD)

    def wide(e):
        return pl.ds(pl.multiple_of(e * PAIR, PAIR), PAIR)

    def ret_copy(gi, j):
        return remote(ret_send.at[gi, j], ret.at[gi, j], r_send.at[gi, j], r_recv.at[gi, j], at(px, py - j, core))

    def back_copy(gi):
        return remote(fwd_stage.at[gi], back.at[gi], b_send.at[gi], b_recv.at[gi], x_prev)

    for gi in range(GROUPS):
        for j in range(SLOTS):
            if j:
                y_copy(gi, j, kv.at[gi, 0]).wait_recv()

            def first(e, _):
                cols = head_cols(gi, e)
                s = dot(kv[gi, j, 0], q_s[:, cols], NT)
                w = jnp.exp2(s * LOG2_FACTOR + bias[j])
                dp = dot(kv[gi, j, 1], g_s[:, cols], NT)
                l = w.reshape(PAIR // 8, 8, PAIR).sum(0)
                d = (w * dp).reshape(PAIR // 8, 8, PAIR).sum(0)
                if j:
                    l_s[e] += l
                    d_s[e] += d
                else:
                    l_s[e] = l
                    d_s[e] = d
                w_s[j, e] = w
                dp_s[j, e] = dp
                return 0

            lax.fori_loop(0, GROUP, first, 0, unroll=2)
            kt_s[:, j * PAIR : (j + 1) * PAIR] = kv[gi, j, 0].T

        def stats(e, _):
            r = 1.0 / l_s[e].sum(0, keepdims=True)
            d = d_s[e].sum(0, keepdims=True) * r
            l_s[e] = jnp.broadcast_to(r, (8, PAIR))
            d_s[e] = jnp.broadcast_to(d, (8, PAIR))
            return 0

        lax.fori_loop(0, GROUP, stats, 0, unroll=True)

        for j in (3, 2, 1, 0):
            dk = jnp.zeros((PAIR, HEAD), F32)
            dv = jnp.zeros((PAIR, HEAD), F32)
            for e in range(GROUP):
                cols = head_cols(gi, e)
                p = w_s[j, e] * l_s[e, :1]
                ds = (p * (dp_s[j, e] - d_s[e, :1])).astype(BF16)
                ds_s[e, j * PAIR : (j + 1) * PAIR] = ds
                dv = dv + dot(p.astype(BF16), g_s[:, cols], NN)
                dk = dk + dot(ds, q_s[:, cols], NN)
            if j:
                ret_send[gi, j, 0] = dk.astype(BF16)
                ret_send[gi, j, 1] = dv.astype(BF16)
                ret_copy(gi, j).start()
            else:
                own[gi, 0] = dk
                own[gi, 1] = dv

        def last(e, _):
            dqt = dot(kt_s[...], ds_s[e], NN) * FACTOR
            dq_s[:, head_cols(gi, e)] = dqt.astype(BF16).T
            return 0

        lax.fori_loop(0, GROUP, last, 0, unroll=2)

    dq_local = pltpu.make_async_copy(dq_s.at[mine], dq_hbm.at[:, my_heads], dq_sem)
    dq_swap = remote(dq_s.at[theirs], dq_hbm.at[:, my_heads], dq_send, dq_recv, sibling)
    dq_local.start()
    dq_swap.start()

    outs = []
    for gi in range(GROUPS):
        for j in range(1, SLOTS):
            ret_copy(gi, j).wait_recv()

        @pl.when(py > 0)
        def _():
            total = jnp.zeros((2, PAIR, HEAD), F32)
            for j in range(1, SLOTS):
                total = total + jnp.where(py + j >= SIDE, ret[gi, j].astype(F32), 0.0)
            fwd_stage[gi] = total.astype(BF16)
            back_copy(gi).start()

    for gi in range(GROUPS):
        total = own[gi]
        for j in range(1, SLOTS):
            total = total + jnp.where(py + j < SIDE, ret[gi, j].astype(F32), 0.0)
        own[gi] = total

        @pl.when(py > 0)
        def _():
            back_copy(gi).wait_recv()
            own[gi] += back[gi].astype(F32)

        out_stage[gi, 0] = (own[gi, 0] * FACTOR).astype(BF16)
        out_stage[gi, 1] = own[gi, 1].astype(BF16)
        for t, dst in enumerate((dk_hbm, dv_hbm)):
            cols = group_cols(core, gi)
            keep = pltpu.make_async_copy(out_stage.at[gi, t, mine], dst.at[:, cols], o_sem.at[gi, t])
            give = remote(out_stage.at[gi, t, theirs], dst.at[:, cols], o_send.at[gi, t], o_recv.at[gi, t], sibling)
            keep.start()
            give.start()
            outs.append((keep, give))

    for keep, give in outs:
        keep.wait()
        give.wait()
    dq_local.wait()
    dq_swap.wait()
    for cp in kv_swap + q_swap:
        cp.wait_send()
    for gi in range(GROUPS):
        for j in range(1, SLOTS):
            y_copy(gi, j, kv.at[gi, 0]).wait_send()
            ret_copy(gi, j).wait_send()

        @pl.when(py > 0)
        def _():
            x_copy(gi).wait_send()
            back_copy(gi).wait_send()


def shards(queries, keys, values, grads, lengths):
    q, k, v, g = queries[0], keys[0], values[0], grads[0]
    vmem = pltpu.VMEM
    dma = pltpu.SemaphoreType.DMA
    hbm = pl.BlockSpec(memory_space=pl.ANY)
    dq, dk, dv = pl.pallas_call(
        kernel,
        out_shape=[jax.ShapeDtypeStruct(a.shape, BF16) for a in (q, k, v)],
        in_specs=[pl.BlockSpec(memory_space=pltpu.SMEM)] + [hbm] * 4,
        out_specs=[hbm] * 3,
        scratch_shapes=[
            vmem((PAIR, GROUPS * GROUP * HEAD), BF16),
            vmem((PAIR, GROUPS * GROUP * HEAD), BF16),
            vmem((GROUPS, SLOTS, 2, PAIR, HEAD), BF16),
            vmem((GROUPS, 2, PAIR, HEAD), BF16),
            vmem((SLOTS, PAIR, PAIR), F32),
            vmem((SLOTS, GROUP, PAIR, PAIR), F32),
            vmem((SLOTS, GROUP, PAIR, PAIR), F32),
            vmem((GROUP, 8, PAIR), F32),
            vmem((GROUP, 8, PAIR), F32),
            vmem((8, 128), F32),
            vmem((GROUP, SLOTS * PAIR, PAIR), BF16),
            vmem((GROUPS, 2, PAIR, HEAD), F32),
            vmem((GROUPS, 2, PAIR, HEAD), BF16),
            vmem((GROUPS, SLOTS, 2, PAIR, HEAD), BF16),
            vmem((GROUPS, SLOTS, 2, PAIR, HEAD), BF16),
            vmem((GROUPS, 2, PAIR, HEAD), BF16),
            vmem((GROUPS, 2, PAIR, HEAD), BF16),
            vmem((PAIR, GROUPS * GROUP * HEAD), BF16),
            vmem((HEAD, SLOTS * PAIR), BF16),
            dma((3, 2)),
            dma((2, GROUPS, 2)),
            dma((GROUPS, 2)),
            dma((GROUPS, SLOTS)), dma((GROUPS, SLOTS)),
            dma((GROUPS,)), dma((GROUPS,)),
            dma((GROUPS, SLOTS)), dma((GROUPS, SLOTS)),
            dma((GROUPS,)), dma((GROUPS,)),
            dma((GROUPS, 2)), dma((GROUPS, 2)), dma((GROUPS, 2)),
            dma, dma, dma,
        ],
        compiler_params=pltpu.CompilerParams(
            collective_id=0, has_side_effects=True, vmem_limit_bytes=56 << 20
        ),
    )(lengths, q, k, v, g)
    return dq[None], dk[None], dv[None]


def solution(mesh):
    spec = P("dp", "ctx", None)
    return jax.shard_map(
        shards,
        mesh=mesh,
        in_specs=(spec, spec, spec, spec, P()),
        out_specs=(spec, spec, spec),
        check_vma=False,
    )
```

profile of v0, /device:TPU:81, one launch (start us, length us, event | category | flops | bytes accessed | tf_op | source)
XLA Modules:
  0.0 55.7 jit_solution(11612994538019290678)
XLA Ops:
  0.6 51.1 %shard_map.76 = (bf16[128,4096]{1,0:T(8,128)(2,1)}, bf16[128,512]{1,0:T(8,128)(2,1)}, bf16[128,512]{1,0:T(8,128)(2,1)}) custom-call(s32[4,16]{1,0:T(4,128)} %lengths.1, bf16[128,4096]{1,0:T(8,128)(2,1)} %bitcast.8, bf16[128,512]{1,0:T(8,128)(2,1)} %bitcast.12, bf16[128,512]{1,0:T(8,128)(2,1)} %bitcast.13, bf16[128,4096]{1,0:T(8,128)(2,1)} %bitcast.9), custom_call_target="tpu_custom_call" | custom-call | tf_op jit(solution)/shard_map/pallas_call | solution.py:278
  51.7 0.0 copy-start.1
  51.7 2.3 %copy.11 = bf16[1,128,4096]{2,1,0:T(8,128)(2,1)} copy(bf16[1,128,4096]{2,1,0:T(8,128)(2,1)} %bitcast.7) | data formatting | bytes 2097152
  54.0 0.0 copy-done.1
  54.1 0.0 copy-start
  54.1 0.7 %copy.12 = bf16[1,128,512]{2,1,0:T(8,128)(2,1)} copy(bf16[1,128,512]{2,1,0:T(8,128)(2,1)S(1)} %bitcast.11) | data formatting | bytes 262144
  54.7 0.3 copy-done
  55.0 0.7 %copy.13 = bf16[1,128,512]{2,1,0:T(8,128)(2,1)} copy(bf16[1,128,512]{2,1,0:T(8,128)(2,1)S(1)} %bitcast.10) | data formatting | bytes 262144
Async XLA Ops:
  51.7 2.3 %copy-start.1 = (bf16[128,512]{1,0:T(8,128)(2,1)S(1)}, bf16[128,512]{1,0:T(8,128)(2,1)}, u32[]{:S(2)}) copy-start(bf16[128,512]{1,0:T(8,128)(2,1)} %get-tuple-element.7) | copy-start | bytes 393220
  54.1 1.0 %copy-start = (bf16[128,512]{1,0:T(8,128)(2,1)S(1)}, bf16[128,512]{1,0:T(8,128)(2,1)}, u32[]{:S(2)}) copy-start(bf16[128,512]{1,0:T(8,128)(2,1)} %get-tuple-element.8) | copy-start | bytes 393220
where the time goes:
time: 55.8 us; the launch traced here: 55.7 us
  Pallas kernels  51.1 us (92%)
  local copies, waits for them, and re-layouts  3.93 us (7%)
  between operations  0.65 us (1%)
    pallas_call x1, Pallas kernels, shards(): pl.pallas_call(kernel, out_shape=[jax.ShapeDtypeStruct(a.shape, BF16) for...  51.1 us
    unnamed x7, local copies, waits for them, and re-layouts  3.93 us

commit v1 on v0

v1 whole, which is shorter than its diff:
```python
import math

import jax
import jax.numpy as jnp
from jax import lax
from jax.experimental import pallas as pl
from jax.experimental.pallas import tpu as pltpu
from jax.sharding import PartitionSpec as P

HEAD = 128
ROWS = 128
PAIR = 2 * ROWS
GROUP = 8
GROUPS = 2
SIDE = 4
DOCS = 16
SLOTS = 4
FACTOR = 1.0 / math.sqrt(HEAD)
LOG2_FACTOR = FACTOR * math.log2(math.e)
BF16 = jnp.bfloat16
F32 = jnp.float32
NT = (((1,), (1,)), ((), ()))
NN = (((1,), (0,)), ((), ()))


def dot(a, b, dims):
    return lax.dot_general(a, b, dims, preferred_element_type=F32)


def kernel(
    lengths, q_hbm, k_hbm, v_hbm, g_hbm,
    dq_hbm, dk_hbm, dv_hbm,
    q_s, g_s, stage, kv, bias, w_s, dp_s, l_s, d_s, ds_s, ret_send, ret, own, own_rx, out_s, dq_s, kt_s,
    ql_sem, q_send, q_recv, st_sem, own_sem, kv_send, kv_recv, f_send, r_send, r_recv, b_send, o_send, o_recv,
    out_sem, dq_sem, dq_send, dq_recv,
):
    dp_at = lax.axis_index("dp")
    me = lax.axis_index("ctx")
    chip, core = me // 2, me % 2
    py = chip % SIDE
    other = 1 - core
    chips = SIDE * SIDE

    def at(c, k):
        return {"ctx": ((c + chips) % chips) * 2 + k}

    sibling = at(chip, other)

    def remote(src, dst, send, recv, where):
        return pltpu.make_async_remote_copy(
            src_ref=src, dst_ref=dst, send_sem=send, recv_sem=recv,
            device_id=where, device_id_type=pl.DeviceIdType.MESH,
        )

    def rows_of(k):
        return pl.ds(pl.multiple_of(k * ROWS, ROWS), ROWS)

    mine, theirs = rows_of(core), rows_of(other)
    half = GROUPS * GROUP * HEAD
    my_heads = pl.ds(pl.multiple_of(core * half, HEAD), half)

    def group_cols(k, gi):
        return pl.ds(pl.multiple_of((k * GROUPS + gi) * HEAD, HEAD), HEAD)

    def query_cols(k, gi):
        return pl.ds(pl.multiple_of((k * GROUPS + gi) * GROUP * HEAD, HEAD), GROUP * HEAD)

    staged = []
    for gi in range(GROUPS):
        for h in range(2):
            for t, src in enumerate((k_hbm, v_hbm)):
                cp = pltpu.make_async_copy(src.at[:, group_cols(h, gi)], stage.at[h, gi, t], st_sem.at[h, gi, t])
                cp.start()
                staged.append(cp)
    owned = []
    for gi in range(GROUPS):
        for t, src in enumerate((k_hbm, v_hbm)):
            cp = pltpu.make_async_copy(src.at[:, group_cols(core, gi)], kv.at[gi, 0, t, mine], own_sem.at[gi, t])
            cp.start()
            owned.append(cp)
    q_local = []
    for gi in range(GROUPS):
        for t, (src, dst) in enumerate(((q_hbm, q_s), (g_hbm, g_s))):
            cp = pltpu.make_async_copy(src.at[:, query_cols(core, gi)], dst.at[gi, mine], ql_sem.at[gi, t])
            cp.start()
            q_local.append(cp)

    barrier = pltpu.get_barrier_semaphore()
    peers = [sibling] + [at(chip + d, k) for j in range(1, SLOTS) for d in (j, -j) for k in range(2)]
    peers += [at(chip + SIDE, core), at(chip - SIDE, core)]
    for peer in peers:
        pl.semaphore_signal(barrier, inc=1, device_id=peer, device_id_type=pl.DeviceIdType.MESH)
    pl.semaphore_wait(barrier, len(peers))
    for cp in staged:
        cp.wait()

    def kv_copy(gi, j, h):
        if j == 1:
            wraps = py == SIDE - 1
            to, slot = jnp.where(wraps, chip - (SIDE - 1), chip + 1), jnp.where(wraps, SLOTS, 1)
        else:
            to, slot = chip + j, j
        return remote(
            stage.at[h, gi], kv.at[gi, slot, :, mine], kv_send.at[gi, j, h], kv_recv.at[gi, slot, core], at(to, h)
        )

    def kv_swap(gi):
        return remote(
            stage.at[other, gi], kv.at[gi, 0, :, mine], kv_send.at[gi, 0, 0], kv_recv.at[gi, 0, core], sibling
        )

    def kv_arrived(gi, slot, k):
        return remote(stage.at[0, gi], kv.at[gi, slot, :, rows_of(k)], kv_send.at[gi, 0, 0], kv_recv.at[gi, slot, k], sibling)

    def kv_forward(gi, k):
        return remote(
            kv.at[gi, SLOTS, :, rows_of(k)], kv.at[gi, 1, :, rows_of(k)], f_send.at[gi, k], kv_recv.at[gi, 1, k],
            at(chip + SIDE, core),
        )

    def q_swap(gi, t):
        src, dst = ((q_hbm, q_s), (g_hbm, g_s))[t]
        return remote(src.at[:, query_cols(other, gi)], dst.at[gi, mine], q_send.at[gi, t], q_recv.at[gi, t], sibling)

    def send_kv(gi):
        kv_swap(gi).start()
        for j in range(1, SLOTS):
            for h in range(2):
                kv_copy(gi, j, h).start()

    def forward_kv(gi):
        @pl.when(py == 0)
        def _():
            for k in range(2):
                kv_arrived(gi, SLOTS, k).wait_recv()
                kv_forward(gi, k).start()

    send_kv(0)
    for t in range(2):
        q_swap(0, t).start()
    send_kv(1)
    for t in range(2):
        q_swap(1, t).start()

    q_pos = chip * PAIR + lax.broadcasted_iota(jnp.int32, (8, PAIR), 1)
    start = jnp.zeros((8, PAIR), jnp.int32)
    bound = jnp.int32(0)
    for d in range(DOCS):
        bound = bound + lengths[dp_at, d]
        start = jnp.where(bound <= q_pos, jnp.maximum(start, bound), start)
    start, q_pos = start[:1], q_pos[:1]
    for j in range(SLOTS):
        k_pos = (chip - j) * PAIR + lax.broadcasted_iota(jnp.int32, (PAIR, PAIR), 0)
        bias[j] = jnp.where((k_pos >= start) & (k_pos <= q_pos), 0.0, -1e30)

    def head_cols(e):
        return pl.ds(pl.multiple_of(e * HEAD, HEAD), HEAD)

    def weights(gi, j):
        if j:
            for k in range(2):
                kv_arrived(gi, j, k).wait_recv()
        else:
            for t in range(2):
                owned[2 * gi + t].wait()
                q_local[2 * gi + t].wait()
                q_swap(gi, t).wait_recv()
            kv_arrived(gi, 0, other).wait_recv()

        def first(e, _):
            cols = head_cols(e)
            s = dot(kv[gi, j, 0], q_s[gi, :, cols], NT)
            w = jnp.exp2(s * LOG2_FACTOR + bias[j])
            dp = dot(kv[gi, j, 1], g_s[gi, :, cols], NT)
            l = w.reshape(PAIR // 8, 8, PAIR).sum(0)
            d = (w * dp).reshape(PAIR // 8, 8, PAIR).sum(0)
            if j:
                l_s[gi, e] += l
                d_s[gi, e] += d
            else:
                l_s[gi, e] = l
                d_s[gi, e] = d
            w_s[gi, j, e] = w
            dp_s[gi, j, e] = dp
            return 0

        lax.fori_loop(0, GROUP, first, 0, unroll=2)
        kt_s[gi, :, j * PAIR : (j + 1) * PAIR] = kv[gi, j, 0].T

    def stats(gi):
        for e in range(GROUP):
            r = 1.0 / l_s[gi, e].sum(0, keepdims=True)
            d = d_s[gi, e].sum(0, keepdims=True) * r
            l_s[gi, e] = jnp.broadcast_to(r, (8, PAIR))
            d_s[gi, e] = jnp.broadcast_to(d, (8, PAIR))

    def ret_copy(gi, j, k):
        if j == 1:
            wraps = py == 0
            to, slot = jnp.where(wraps, chip + SIDE - 1, chip - 1), jnp.where(wraps, SLOTS, 1)
        else:
            to, slot = chip - j, j
        return remote(ret_send.at[gi, j, k], ret.at[core, gi, slot], r_send.at[gi, j, k], r_recv.at[core, gi, slot], at(to, k))

    def ret_arrived(h, gi, slot):
        return remote(ret_send.at[gi, 1, 0], ret.at[h, gi, slot], r_send.at[gi, 1, 0], r_recv.at[h, gi, slot], sibling)

    def ret_forward(gi, h):
        return remote(ret.at[h, gi, SLOTS], ret.at[h, gi, 1], b_send.at[gi, h], r_recv.at[h, gi, 1], at(chip - SIDE, core))

    def forward_ret(gi):
        @pl.when(py == SIDE - 1)
        def _():
            for h in range(2):
                ret_arrived(h, gi, SLOTS).wait_recv()
                ret_forward(gi, h).start()

    def own_swap(gi):
        return remote(own.at[gi, :, theirs], own_rx.at[gi], o_send.at[gi], o_recv.at[gi], sibling)

    def terms(gi, j):
        dk = jnp.zeros((PAIR, HEAD), F32)
        dv = jnp.zeros((PAIR, HEAD), F32)
        for e in range(GROUP):
            cols = head_cols(e)
            p = w_s[gi, j, e] * l_s[gi, e, :1]
            ds = (p * (dp_s[gi, j, e] - d_s[gi, e, :1])).astype(BF16)
            ds_s[e, j * PAIR : (j + 1) * PAIR] = ds
            dv = dv + dot(p.astype(BF16), g_s[gi, :, cols], NN)
            dk = dk + dot(ds, q_s[gi, :, cols], NN)
        if j:
            for t, total in enumerate((dk, dv)):
                low = total.astype(BF16)
                for k in range(2):
                    ret_send[gi, j, k, t] = low[k * ROWS : (k + 1) * ROWS]
            for k in range(2):
                ret_copy(gi, j, k).start()
        else:
            own[gi, 0] = dk
            own[gi, 1] = dv
            own_swap(gi).start()

    def dq_local(gi):
        return pltpu.make_async_copy(dq_s.at[gi, mine], dq_hbm.at[:, query_cols(core, gi)], dq_sem.at[gi])

    def dq_swap(gi):
        return remote(dq_s.at[gi, theirs], dq_hbm.at[:, query_cols(core, gi)], dq_send.at[gi], dq_recv.at[gi], sibling)

    def query_grads(gi):
        def last(e, _):
            dqt = dot(kt_s[gi], ds_s[e], NN) * FACTOR
            dq_s[gi, :, head_cols(e)] = dqt.astype(BF16).T
            return 0

        lax.fori_loop(0, GROUP, last, 0, unroll=2)
        dq_local(gi).start()
        dq_swap(gi).start()

    weights(0, 0)
    forward_kv(0)
    weights(1, 0)
    for j in range(1, SLOTS):
        weights(0, j)
    forward_kv(1)
    stats(0)
    for j in (1, 3, 2, 0):
        terms(0, j)
    query_grads(0)
    for j in range(1, SLOTS):
        weights(1, j)
    forward_ret(0)
    stats(1)
    for j in (1, 3, 2, 0):
        terms(1, j)
    forward_ret(1)
    query_grads(1)

    for gi in range(GROUPS):
        for h, mine_too in ((core, True), (other, False)):
            if mine_too:
                total = own[gi, :, mine]
            else:
                own_swap(gi).wait_recv()
                total = own_rx[gi]
            for j in range(1, SLOTS):
                ret_arrived(h, gi, j).wait_recv()
                total = total + ret[h, gi, j].astype(F32)
            out_s[0, :, group_cols(h, gi)] = (total[0] * FACTOR).astype(BF16)
            out_s[1, :, group_cols(h, gi)] = total[1].astype(BF16)
    outs = []
    for t, dst in enumerate((dk_hbm, dv_hbm)):
        cp = pltpu.make_async_copy(out_s.at[t], dst, out_sem.at[t])
        cp.start()
        outs.append(cp)
    for cp in outs:
        cp.wait()
    for gi in range(GROUPS):
        dq_local(gi).wait()
        dq_swap(gi).wait()
        kv_swap(gi).wait_send()
        own_swap(gi).wait_send()
        for t in range(2):
            q_swap(gi, t).wait_send()
        for j in range(1, SLOTS):
            for k in range(2):
                kv_copy(gi, j, k).wait_send()
                ret_copy(gi, j, k).wait_send()

        @pl.when(py == 0)
        def _():
            for k in range(2):
                kv_forward(gi, k).wait_send()

        @pl.when(py == SIDE - 1)
        def _():
            for h in range(2):
                ret_forward(gi, h).wait_send()


def handed_on(dq, dk, dv, dq_out, dk_out, dv_out):
    dq_out[...] = dq[...]
    dk_out[...] = dk[...]
    dv_out[...] = dv[...]


def shards(queries, keys, values, grads, lengths):
    q, k, v, g = queries[0], keys[0], values[0], grads[0]
    vmem = pltpu.VMEM
    dma = pltpu.SemaphoreType.DMA
    hbm = pl.BlockSpec(memory_space=pl.ANY)
    dq, dk, dv = pl.pallas_call(
        kernel,
        out_shape=[jax.ShapeDtypeStruct(a.shape, BF16) for a in (q, k, v)],
        in_specs=[pl.BlockSpec(memory_space=pltpu.SMEM)] + [hbm] * 4,
        out_specs=[hbm] * 3,
        scratch_shapes=[
            vmem((GROUPS, PAIR, GROUP * HEAD), BF16),
            vmem((GROUPS, PAIR, GROUP * HEAD), BF16),
            vmem((2, GROUPS, 2, ROWS, HEAD), BF16),
            vmem((GROUPS, SLOTS + 1, 2, PAIR, HEAD), BF16),
            vmem((SLOTS, PAIR, PAIR), F32),
            vmem((GROUPS, SLOTS, GROUP, PAIR, PAIR), F32),
            vmem((GROUPS, SLOTS, GROUP, PAIR, PAIR), F32),
            vmem((GROUPS, GROUP, 8, PAIR), F32),
            vmem((GROUPS, GROUP, 8, PAIR), F32),
            vmem((GROUP, SLOTS * PAIR, PAIR), BF16),
            vmem((GROUPS, SLOTS, 2, 2, ROWS, HEAD), BF16),
            vmem((2, GROUPS, SLOTS + 1, 2, ROWS, HEAD), BF16),
            vmem((GROUPS, 2, PAIR, HEAD), F32),
            vmem((GROUPS, 2, ROWS, HEAD), F32),
            vmem((2, ROWS, 2 * GROUPS * HEAD), BF16),
            vmem((GROUPS, PAIR, GROUP * HEAD), BF16),
            vmem((GROUPS, HEAD, SLOTS * PAIR), BF16),
            dma((GROUPS, 2)), dma((GROUPS, 2)), dma((GROUPS, 2)),
            dma((2, GROUPS, 2)), dma((GROUPS, 2)),
            dma((GROUPS, SLOTS, 2)), dma((GROUPS, SLOTS + 1, 2)), dma((GROUPS, 2)),
            dma((GROUPS, SLOTS, 2)), dma((2, GROUPS, SLOTS + 1)), dma((GROUPS, 2)),
            dma((GROUPS,)), dma((GROUPS,)),
            dma((2,)), dma((GROUPS,)), dma((GROUPS,)), dma((GROUPS,)),
        ],
        compiler_params=pltpu.CompilerParams(
            collective_id=0, has_side_effects=True, vmem_limit_bytes=60 << 20
        ),
    )(lengths, q, k, v, g)
    steps = 4
    specs = [pl.BlockSpec((ROWS // steps, a.shape[1]), lambda i: (i, 0)) for a in (q, k, v)]
    dq, dk, dv = pl.pallas_call(
        handed_on, grid=(steps,), out_shape=[jax.ShapeDtypeStruct(a.shape, BF16) for a in (q, k, v)],
        in_specs=specs, out_specs=specs,
    )(dq, dk, dv)
    return dq[None], dk[None], dv[None]


def solution(mesh):
    spec = P("dp", "ctx", None)
    return jax.shard_map(
        shards,
        mesh=mesh,
        in_specs=(spec, spec, spec, spec, P()),
        out_specs=(spec, spec, spec),
        check_vma=False,
    )
```

time: 55.8 us -> 48 us (0.86)
  the two profiles are of different devices: /device:TPU:81 before, /device:TPU:121 now
where the time goes in v1:
time: 48 us; the launch traced here: 47.8 us
  Pallas kernels  47.2 us (98%)
  between operations  0.64 us (1%)
    pallas_call x1, Pallas kernels, shards(): pl.pallas_call(kernel, out_shape=[jax.ShapeDtypeStruct(a.shape, BF16) for...  43.7 us
    pallas_call x1, Pallas kernels, shards(): pl.pallas_call(handed_on, grid=(steps,), out_shape=[jax.ShapeDtypeStruct(...  3.46 us

profile of v1, /device:TPU:121, one launch (start us, length us, event | category | flops | bytes accessed | tf_op | source)
XLA Modules:
  0.0 47.8 jit_solution(12100455896810525421)
XLA Ops:
  0.6 43.7 %shard_map.76 = (bf16[128,4096]{1,0:T(8,128)(2,1)}, bf16[128,512]{1,0:T(8,128)(2,1)}, bf16[128,512]{1,0:T(8,128)(2,1)}) custom-call(s32[4,16]{1,0:T(4,128)} %lengths.1, bf16[128,4096]{1,0:T(8,128)(2,1)} %bitcast.7, bf16[128,512]{1,0:T(8,128)(2,1)} %bitcast.9, bf16[128,512]{1,0:T(8,128)(2,1)} %bitcast.10, bf16[128,4096]{1,0:T(8,128)(2,1)} %bitcast.8), custom_call_target="tpu_custom_call" | custom-call | tf_op jit(solution)/shard_map/pallas_call | solution.py:331
  44.4 3.5 %shard_map.77 = (bf16[128,4096]{1,0:T(8,128)(2,1)}, bf16[128,512]{1,0:T(8,128)(2,1)}, bf16[128,512]{1,0:T(8,128)(2,1)}) custom-call(bf16[128,4096]{1,0:T(8,128)(2,1)} %get-tuple-element.9.dq, bf16[128,512]{1,0:T(8,128)(2,1)} %get-tuple-element.10.dk, bf16[128,512]{1,0:T(8,128)(2,1)} %get-tuple-element.11.dv), custom_call_target="tpu_custom_call" | custom-call | tf_op jit(solution)/shard_map/pallas_call | solution.py:367

commit v2 on v1

--- a/solution.py
+++ b/solution.py
@@ -19,7 +19,6 @@
 LOG2_FACTOR = FACTOR * math.log2(math.e)
 BF16 = jnp.bfloat16
 F32 = jnp.float32
-NT = (((1,), (1,)), ((), ()))
 NN = (((1,), (0,)), ((), ()))
 
 
@@ -30,8 +29,8 @@
 def kernel(
     lengths, q_hbm, k_hbm, v_hbm, g_hbm,
     dq_hbm, dk_hbm, dv_hbm,
-    q_s, g_s, stage, kv, bias, w_s, dp_s, l_s, d_s, ds_s, ret_send, ret, own, own_rx, out_s, dq_s, kt_s,
-    ql_sem, q_send, q_recv, st_sem, own_sem, kv_send, kv_recv, f_send, r_send, r_recv, b_send, o_send, o_recv,
+    q_s, g_s, qt_s, gt_s, qh_s, gh_s, stage, kv, bias, w_s, dp_s, l_s, d_s, ds_s, ex_send, ex, held, ret_send, ret, own, own_rx, out_s, dq_s, kt_s,
+    ql_sem, q_send, q_recv, st_sem, own_sem, kv_send, kv_recv, f_send, h_send, e_send, e_recv, r_send, r_recv, b_send, o_send, o_recv,
     out_sem, dq_sem, dq_send, dq_recv,
 ):
     dp_at = lax.axis_index("dp")
@@ -86,7 +85,7 @@
             q_local.append(cp)
 
     barrier = pltpu.get_barrier_semaphore()
-    peers = [sibling] + [at(chip + d, k) for j in range(1, SLOTS) for d in (j, -j) for k in range(2)]
+    peers = [sibling] + [at(chip + d, k) for d in (1, -1, 3, -3) for k in range(2)]
     peers += [at(chip + SIDE, core), at(chip - SIDE, core)]
     for peer in peers:
         pl.semaphore_signal(barrier, inc=1, device_id=peer, device_id_type=pl.DeviceIdType.MESH)
@@ -94,46 +93,60 @@
     for cp in staged:
         cp.wait()
 
-    def kv_copy(gi, j, h):
+    def kv_copy(gi, j, h, t):
         if j == 1:
             wraps = py == SIDE - 1
             to, slot = jnp.where(wraps, chip - (SIDE - 1), chip + 1), jnp.where(wraps, SLOTS, 1)
         else:
             to, slot = chip + j, j
         return remote(
-            stage.at[h, gi], kv.at[gi, slot, :, mine], kv_send.at[gi, j, h], kv_recv.at[gi, slot, core], at(to, h)
-        )
-
-    def kv_swap(gi):
-        return remote(
-            stage.at[other, gi], kv.at[gi, 0, :, mine], kv_send.at[gi, 0, 0], kv_recv.at[gi, 0, core], sibling
-        )
-
-    def kv_arrived(gi, slot, k):
-        return remote(stage.at[0, gi], kv.at[gi, slot, :, rows_of(k)], kv_send.at[gi, 0, 0], kv_recv.at[gi, slot, k], sibling)
-
-    def kv_forward(gi, k):
-        return remote(
-            kv.at[gi, SLOTS, :, rows_of(k)], kv.at[gi, 1, :, rows_of(k)], f_send.at[gi, k], kv_recv.at[gi, 1, k],
+            stage.at[h, gi, t], kv.at[gi, slot, t, mine], kv_send.at[gi, j, h, t], kv_recv.at[gi, slot, t, core], at(to, h)
+        )
+
+    def kv_swap(gi, t):
+        return remote(
+            stage.at[other, gi, t], kv.at[gi, 0, t, mine], kv_send.at[gi, 0, 0, t], kv_recv.at[gi, 0, t, core], sibling
+        )
+
+    def kv_arrived(gi, slot, t, k):
+        return remote(
+            stage.at[0, gi, t], kv.at[gi, slot, t, rows_of(k)], kv_send.at[gi, 0, 0, t], kv_recv.at[gi, slot, t, k], sibling
+        )
+
+    def kv_forward(gi, t, k):
+        return remote(
+            kv.at[gi, SLOTS, t, rows_of(k)], kv.at[gi, 1, t, rows_of(k)], f_send.at[gi, t, k], kv_recv.at[gi, 1, t, k],
             at(chip + SIDE, core),
         )
+
+    def kv_hop(gi, t):
+        slot, to = (1, chip + 1) if t == 0 else (3, chip - 1)
+        return remote(kv.at[gi, slot, t], kv.at[gi, 2, t], h_send.at[gi, t], kv_recv.at[gi, 2, t, 0], at(to, core))
 
     def q_swap(gi, t):
         src, dst = ((q_hbm, q_s), (g_hbm, g_s))[t]
         return remote(src.at[:, query_cols(other, gi)], dst.at[gi, mine], q_send.at[gi, t], q_recv.at[gi, t], sibling)
 
     def send_kv(gi):
-        kv_swap(gi).start()
-        for j in range(1, SLOTS):
+        for t in range(2):
+            kv_swap(gi, t).start()
+        for t, j in ((0, 1), (1, 3), (1, 1), (0, 3)):
             for h in range(2):
-                kv_copy(gi, j, h).start()
+                kv_copy(gi, j, h, t).start()
 
     def forward_kv(gi):
         @pl.when(py == 0)
         def _():
+            for t in range(2):
+                for k in range(2):
+                    kv_arrived(gi, SLOTS, t, k).wait_recv()
+                    kv_forward(gi, t, k).start()
+
+    def hop_kv(gi):
+        for t, slot in ((1, 3), (0, 1)):
             for k in range(2):
-                kv_arrived(gi, SLOTS, k).wait_recv()
-                kv_forward(gi, k).start()
+                kv_arrived(gi, slot, t, k).wait_recv()
+            kv_hop(gi, t).start()
 
     send_kv(0)
     for t in range(2):
@@ -157,21 +170,30 @@
         return pl.ds(pl.multiple_of(e * HEAD, HEAD), HEAD)
 
     def weights(gi, j):
-        if j:
+        if j == 2:
+            for t in range(2):
+                kv_hop(gi, t).wait_recv()
+        elif j:
             for k in range(2):
-                kv_arrived(gi, j, k).wait_recv()
+                kv_arrived(gi, j, 1 if j == 1 else 0, k).wait_recv()
         else:
             for t in range(2):
                 owned[2 * gi + t].wait()
                 q_local[2 * gi + t].wait()
                 q_swap(gi, t).wait_recv()
-            kv_arrived(gi, 0, other).wait_recv()
+                kv_arrived(gi, 0, t, other).wait_recv()
+            for e in range(GROUP):
+                cols = slice(e * HEAD, (e + 1) * HEAD)
+                at_e = slice(e * PAIR, (e + 1) * PAIR)
+                for src, flat, turned in ((q_s, qh_s, qt_s), (g_s, gh_s, gt_s)):
+                    block = src[gi, :, cols]
+                    flat[gi, at_e] = block
+                    turned[gi, e] = block.T
 
         def first(e, _):
-            cols = head_cols(e)
-            s = dot(kv[gi, j, 0], q_s[gi, :, cols], NT)
+            s = dot(kv[gi, j, 0], qt_s[gi, e], NN)
             w = jnp.exp2(s * LOG2_FACTOR + bias[j])
-            dp = dot(kv[gi, j, 1], g_s[gi, :, cols], NT)
+            dp = dot(kv[gi, j, 1], gt_s[gi, e], NN)
             l = w.reshape(PAIR // 8, 8, PAIR).sum(0)
             d = (w * dp).reshape(PAIR // 8, 8, PAIR).sum(0)
             if j:
@@ -184,7 +206,7 @@
             dp_s[gi, j, e] = dp
             return 0
 
-        lax.fori_loop(0, GROUP, first, 0, unroll=2)
+        lax.fori_loop(0, GROUP, first, 0, unroll=8)
         kt_s[gi, :, j * PAIR : (j + 1) * PAIR] = kv[gi, j, 0].T
 
     def stats(gi):
@@ -194,51 +216,73 @@
             l_s[gi, e] = jnp.broadcast_to(r, (8, PAIR))
             d_s[gi, e] = jnp.broadcast_to(d, (8, PAIR))
 
-    def ret_copy(gi, j, k):
+    def ret_copy(gi, j, t, k):
         if j == 1:
             wraps = py == 0
             to, slot = jnp.where(wraps, chip + SIDE - 1, chip - 1), jnp.where(wraps, SLOTS, 1)
         else:
             to, slot = chip - j, j
-        return remote(ret_send.at[gi, j, k], ret.at[core, gi, slot], r_send.at[gi, j, k], r_recv.at[core, gi, slot], at(to, k))
-
-    def ret_arrived(h, gi, slot):
-        return remote(ret_send.at[gi, 1, 0], ret.at[h, gi, slot], r_send.at[gi, 1, 0], r_recv.at[h, gi, slot], sibling)
-
-    def ret_forward(gi, h):
-        return remote(ret.at[h, gi, SLOTS], ret.at[h, gi, 1], b_send.at[gi, h], r_recv.at[h, gi, 1], at(chip - SIDE, core))
+        return remote(
+            ret_send.at[gi, j, t, k], ret.at[core, gi, slot, t], r_send.at[gi, j, t, k], r_recv.at[core, gi, slot, t], at(to, k)
+        )
+
+    def ret_arrived(h, gi, slot, t):
+        return remote(ret_send.at[gi, 1, t, 0], ret.at[h, gi, slot, t], r_send.at[gi, 1, t, 0], r_recv.at[h, gi, slot, t], sibling)
+
+    def ret_forward(gi, t, h):
+        return remote(
+            ret.at[h, gi, SLOTS, t], ret.at[h, gi, 1, t], b_send.at[gi, t, h], r_recv.at[h, gi, 1, t], at(chip - SIDE, core)
+        )
 
     def forward_ret(gi):
         @pl.when(py == SIDE - 1)
         def _():
-            for h in range(2):
-                ret_arrived(h, gi, SLOTS).wait_recv()
-                ret_forward(gi, h).start()
+            for t in (1, 0):
+                for h in range(2):
+                    ret_arrived(h, gi, SLOTS, t).wait_recv()
+                    ret_forward(gi, t, h).start()
+
+    def ex_copy(gi, t):
+        return remote(ex_send.at[gi, t], ex.at[gi, t], e_send.at[gi, t], e_recv.at[gi, t], at(chip - 1 if t == 0 else chip + 1, core))
+
+    def send_terms(gi, j, t, total):
+        low = total.astype(BF16)
+        for k in range(2):
+            ret_send[gi, j, t, k] = low[k * ROWS : (k + 1) * ROWS]
+            ret_copy(gi, j, t, k).start()
 
     def own_swap(gi):
         return remote(own.at[gi, :, theirs], own_rx.at[gi], o_send.at[gi], o_recv.at[gi], sibling)
 
     def terms(gi, j):
-        dk = jnp.zeros((PAIR, HEAD), F32)
-        dv = jnp.zeros((PAIR, HEAD), F32)
-        for e in range(GROUP):
-            cols = head_cols(e)
-            p = w_s[gi, j, e] * l_s[gi, e, :1]
-            ds = (p * (dp_s[gi, j, e] - d_s[gi, e, :1])).astype(BF16)
-            ds_s[e, j * PAIR : (j + 1) * PAIR] = ds
-            dv = dv + dot(p.astype(BF16), g_s[gi, :, cols], NN)
-            dk = dk + dot(ds, q_s[gi, :, cols], NN)
-        if j:
-            for t, total in enumerate((dk, dv)):
-                low = total.astype(BF16)
-                for k in range(2):
-                    ret_send[gi, j, k, t] = low[k * ROWS : (k + 1) * ROWS]
-            for k in range(2):
-                ret_copy(gi, j, k).start()
-        else:
-            own[gi, 0] = dk
-            own[gi, 1] = dv
-            own_swap(gi).start()
+        rows = slice(j * PAIR, (j + 1) * PAIR)
+        dk = dv = None
+        for e0 in range(0, GROUP, 2):
+            low = []
+            for e in range(e0, e0 + 2):
+                p = w_s[gi, j, e] * l_s[gi, e, :1]
+                ds_s[gi, rows, e * PAIR : (e + 1) * PAIR] = (p * (dp_s[gi, j, e] - d_s[gi, e, :1])).astype(BF16)
+                low.append(p.astype(BF16))
+            part = slice(e0 * PAIR, (e0 + 2) * PAIR)
+            dv_part = dot(jnp.concatenate(low, axis=1), gh_s[gi, part], NN)
+            dk_part = dot(ds_s[gi, rows, part], qh_s[gi, part], NN)
+            dv = dv_part if dv is None else dv + dv_part
+            dk = dk_part if dk is None else dk + dk_part
+        return dk, dv
+
+    def all_terms(gi):
+        for t, total in enumerate(terms(gi, 2)):
+            ex_send[gi, t] = total.astype(BF16)
+            ex_copy(gi, t).start()
+        held[0], dv = terms(gi, 1)
+        send_terms(gi, 1, 1, dv)
+        dk, held[1] = terms(gi, 3)
+        send_terms(gi, 3, 0, dk)
+        for t in range(2):
+            ex_copy(gi, t).wait_recv()
+            send_terms(gi, (1, 3)[t], t, held[t] + ex[gi, t].astype(F32))
+        own[gi, 0], own[gi, 1] = terms(gi, 0)
+        own_swap(gi).start()
 
     def dq_local(gi):
         return pltpu.make_async_copy(dq_s.at[gi, mine], dq_hbm.at[:, query_cols(core, gi)], dq_sem.at[gi])
@@ -248,30 +292,31 @@
 
     def query_grads(gi):
         def last(e, _):
-            dqt = dot(kt_s[gi], ds_s[e], NN) * FACTOR
+            dqt = dot(kt_s[gi], ds_s[gi, :, pl.ds(pl.multiple_of(e * PAIR, PAIR), PAIR)], NN) * FACTOR
             dq_s[gi, :, head_cols(e)] = dqt.astype(BF16).T
             return 0
 
-        lax.fori_loop(0, GROUP, last, 0, unroll=2)
+        lax.fori_loop(0, GROUP, last, 0, unroll=8)
         dq_local(gi).start()
         dq_swap(gi).start()
 
     weights(0, 0)
     forward_kv(0)
     weights(1, 0)
-    for j in range(1, SLOTS):
-        weights(0, j)
+    hop_kv(0)
     forward_kv(1)
+    weights(0, 1)
+    weights(0, 3)
+    hop_kv(1)
+    weights(0, 2)
     stats(0)
-    for j in (1, 3, 2, 0):
-        terms(0, j)
-    query_grads(0)
-    for j in range(1, SLOTS):
+    all_terms(0)
+    for j in (1, 3, 2):
         weights(1, j)
     forward_ret(0)
     stats(1)
-    for j in (1, 3, 2, 0):
-        terms(1, j)
+    all_terms(1)
+    query_grads(0)
     forward_ret(1)
     query_grads(1)
 
@@ -282,8 +327,9 @@
             else:
                 own_swap(gi).wait_recv()
                 total = own_rx[gi]
-            for j in range(1, SLOTS):
-                ret_arrived(h, gi, j).wait_recv()
+            for j in (3, 1):
+                for t in range(2):
+                    ret_arrived(h, gi, j, t).wait_recv()
                 total = total + ret[h, gi, j].astype(F32)
             out_s[0, :, group_cols(h, gi)] = (total[0] * FACTOR).astype(BF16)
             out_s[1, :, group_cols(h, gi)] = total[1].astype(BF16)
@@ -297,24 +343,28 @@
     for gi in range(GROUPS):
         dq_local(gi).wait()
         dq_swap(gi).wait()
-        kv_swap(gi).wait_send()
         own_swap(gi).wait_send()
         for t in range(2):
             q_swap(gi, t).wait_send()
-        for j in range(1, SLOTS):
-            for k in range(2):
-                kv_copy(gi, j, k).wait_send()
-                ret_copy(gi, j, k).wait_send()
+            kv_swap(gi, t).wait_send()
+            kv_hop(gi, t).wait_send()
+            ex_copy(gi, t).wait_send()
+            for j in (1, 3):
+                for k in range(2):
+                    kv_copy(gi, j, k, t).wait_send()
+                    ret_copy(gi, j, t, k).wait_send()
 
         @pl.when(py == 0)
         def _():
-            for k in range(2):
-                kv_forward(gi, k).wait_send()
+            for t in range(2):
+                for k in range(2):
+                    kv_forward(gi, t, k).wait_send()
 
         @pl.when(py == SIDE - 1)
         def _():
-            for h in range(2):
-                ret_forward(gi, h).wait_send()
+            for t in range(2):
+                for h in range(2):
+                    ret_forward(gi, t, h).wait_send()
 
 
 def handed_on(dq, dk, dv, dq_out, dk_out, dv_out):
@@ -336,6 +386,10 @@
         scratch_shapes=[
             vmem((GROUPS, PAIR, GROUP * HEAD), BF16),
             vmem((GROUPS, PAIR, GROUP * HEAD), BF16),
+            vmem((GROUPS, GROUP, HEAD, PAIR), BF16),
+            vmem((GROUPS, GROUP, HEAD, PAIR), BF16),
+            vmem((GROUPS, GROUP * PAIR, HEAD), BF16),
+            vmem((GROUPS, GROUP * PAIR, HEAD), BF16),
             vmem((2, GROUPS, 2, ROWS, HEAD), BF16),
             vmem((GROUPS, SLOTS + 1, 2, PAIR, HEAD), BF16),
             vmem((SLOTS, PAIR, PAIR), F32),
@@ -343,7 +397,10 @@
             vmem((GROUPS, SLOTS, GROUP, PAIR, PAIR), F32),
             vmem((GROUPS, GROUP, 8, PAIR), F32),
             vmem((GROUPS, GROUP, 8, PAIR), F32),
-            vmem((GROUP, SLOTS * PAIR, PAIR), BF16),
+            vmem((GROUPS, SLOTS * PAIR, GROUP * PAIR), BF16),
+            vmem((GROUPS, 2, PAIR, HEAD), BF16),
+            vmem((GROUPS, 2, PAIR, HEAD), BF16),
+            vmem((2, PAIR, HEAD), F32),
             vmem((GROUPS, SLOTS, 2, 2, ROWS, HEAD), BF16),
             vmem((2, GROUPS, SLOTS + 1, 2, ROWS, HEAD), BF16),
             vmem((GROUPS, 2, PAIR, HEAD), F32),
@@ -353,8 +410,9 @@
             vmem((GROUPS, HEAD, SLOTS * PAIR), BF16),
             dma((GROUPS, 2)), dma((GROUPS, 2)), dma((GROUPS, 2)),
             dma((2, GROUPS, 2)), dma((GROUPS, 2)),
-            dma((GROUPS, SLOTS, 2)), dma((GROUPS, SLOTS + 1, 2)), dma((GROUPS, 2)),
-            dma((GROUPS, SLOTS, 2)), dma((2, GROUPS, SLOTS + 1)), dma((GROUPS, 2)),
+            dma((GROUPS, SLOTS, 2, 2)), dma((GROUPS, SLOTS + 1, 2, 2)), dma((GROUPS, 2, 2)), dma((GROUPS, 2)),
+            dma((GROUPS, 2)), dma((GROUPS, 2)),
+            dma((GROUPS, SLOTS, 2, 2)), dma((2, GROUPS, SLOTS + 1, 2)), dma((GROUPS, 2, 2)),
             dma((GROUPS,)), dma((GROUPS,)),
             dma((2,)), dma((GROUPS,)), dma((GROUPS,)), dma((GROUPS,)),
         ],
@@ -362,7 +420,7 @@
             collective_id=0, has_side_effects=True, vmem_limit_bytes=60 << 20
         ),
     )(lengths, q, k, v, g)
-    steps = 4
+    steps = 2
     specs = [pl.BlockSpec((ROWS // steps, a.shape[1]), lambda i: (i, 0)) for a in (q, k, v)]
     dq, dk, dv = pl.pallas_call(
         handed_on, grid=(steps,), out_shape=[jax.ShapeDtypeStruct(a.shape, BF16) for a in (q, k, v)],

time: 48 us -> 42.6 us (0.89)
  the two profiles are of different devices: /device:TPU:121 before, /device:TPU:1 now
where the time goes in v2:
time: 42.6 us; the launch traced here: 42.5 us
  Pallas kernels  41.8 us (98%)
  between operations  0.64 us (2%)
    pallas_call x1, Pallas kernels, shards(): pl.pallas_call(kernel, out_shape=[jax.ShapeDtypeStruct(a.shape, BF16) for...  39.7 us
    pallas_call x1, Pallas kernels, shards(): pl.pallas_call(handed_on, grid=(steps,), out_shape=[jax.ShapeDtypeStruct(...  2.18 us

profile of v2, /device:TPU:1, one launch (start us, length us, event | category | flops | bytes accessed | tf_op | source)
XLA Modules:
  0.0 42.5 jit_solution(5945140187193962458)
XLA Ops:
  0.6 39.7 %shard_map.76 = (bf16[128,4096]{1,0:T(8,128)(2,1)}, bf16[128,512]{1,0:T(8,128)(2,1)}, bf16[128,512]{1,0:T(8,128)(2,1)}) custom-call(s32[4,16]{1,0:T(4,128)} %lengths.1, bf16[128,4096]{1,0:T(8,128)(2,1)} %bitcast.7, bf16[128,512]{1,0:T(8,128)(2,1)} %bitcast.9, bf16[128,512]{1,0:T(8,128)(2,1)} %bitcast.10, bf16[128,4096]{1,0:T(8,128)(2,1)} %bitcast.8), custom_call_target="tpu_custom_call" | custom-call | tf_op jit(solution)/shard_map/pallas_call | solution.py:381
  40.3 2.2 %shard_map.77 = (bf16[128,4096]{1,0:T(8,128)(2,1)}, bf16[128,512]{1,0:T(8,128)(2,1)}, bf16[128,512]{1,0:T(8,128)(2,1)}) custom-call(bf16[128,4096]{1,0:T(8,128)(2,1)} %get-tuple-element.9.dq, bf16[128,512]{1,0:T(8,128)(2,1)} %get-tuple-element.10.dk, bf16[128,512]{1,0:T(8,128)(2,1)} %get-tuple-element.11.dv), custom_call_target="tpu_custom_call" | custom-call | tf_op jit(solution)/shard_map/pallas_call | solution.py:425

commit v3 on v2

--- a/solution.py
+++ b/solution.py
@@ -17,6 +17,8 @@
 SLOTS = 4
 FACTOR = 1.0 / math.sqrt(HEAD)
 LOG2_FACTOR = FACTOR * math.log2(math.e)
+KV_HOPS = (0, 1)
+TERM_HOPS = (0, 1)
 BF16 = jnp.bfloat16
 F32 = jnp.float32
 NN = (((1,), (0,)), ((), ()))
@@ -130,7 +132,9 @@
     def send_kv(gi):
         for t in range(2):
             kv_swap(gi, t).start()
-        for t, j in ((0, 1), (1, 3), (1, 1), (0, 3)):
+        for t, j in ((0, 1), (1, 3), (1, 1), (0, 3), (0, 2), (1, 2)):
+            if j == 2 and gi in KV_HOPS:
+                continue
             for h in range(2):
                 kv_copy(gi, j, h, t).start()
 
@@ -146,7 +150,8 @@
         for t, slot in ((1, 3), (0, 1)):
             for k in range(2):
                 kv_arrived(gi, slot, t, k).wait_recv()
-            kv_hop(gi, t).start()
+            if gi in KV_HOPS:
+                kv_hop(gi, t).start()
 
     send_kv(0)
     for t in range(2):
@@ -172,7 +177,11 @@
     def weights(gi, j):
         if j == 2:
             for t in range(2):
-                kv_hop(gi, t).wait_recv()
+                if gi in KV_HOPS:
+                    kv_hop(gi, t).wait_recv()
+                else:
+                    for k in range(2):
+                        kv_arrived(gi, 2, t, k).wait_recv()
         elif j:
             for k in range(2):
                 kv_arrived(gi, j, 1 if j == 1 else 0, k).wait_recv()
@@ -270,17 +279,24 @@
             dk = dk_part if dk is None else dk + dk_part
         return dk, dv
 
-    def all_terms(gi):
-        for t, total in enumerate(terms(gi, 2)):
-            ex_send[gi, t] = total.astype(BF16)
-            ex_copy(gi, t).start()
-        held[0], dv = terms(gi, 1)
-        send_terms(gi, 1, 1, dv)
-        dk, held[1] = terms(gi, 3)
-        send_terms(gi, 3, 0, dk)
-        for t in range(2):
-            ex_copy(gi, t).wait_recv()
-            send_terms(gi, (1, 3)[t], t, held[t] + ex[gi, t].astype(F32))
+    def all_terms(gi, between=None):
+        if gi in TERM_HOPS:
+            for t, total in enumerate(terms(gi, 2)):
+                ex_send[gi, t] = total.astype(BF16)
+                ex_copy(gi, t).start()
+            held[0], dv = terms(gi, 1)
+            send_terms(gi, 1, 1, dv)
+            if between is not None:
+                between()
+            dk, held[1] = terms(gi, 3)
+            send_terms(gi, 3, 0, dk)
+            for t in range(2):
+                ex_copy(gi, t).wait_recv()
+                send_terms(gi, (1, 3)[t], t, held[t] + ex[gi, t].astype(F32))
+        else:
+            for j in (1, 2, 3):
+                for t, total in enumerate(terms(gi, j)):
+                    send_terms(gi, j, t, total)
         own[gi, 0], own[gi, 1] = terms(gi, 0)
         own_swap(gi).start()
 
@@ -307,17 +323,16 @@
     forward_kv(1)
     weights(0, 1)
     weights(0, 3)
-    hop_kv(1)
     weights(0, 2)
     stats(0)
-    all_terms(0)
+    all_terms(0, lambda: hop_kv(1))
     for j in (1, 3, 2):
         weights(1, j)
     forward_ret(0)
     stats(1)
     all_terms(1)
+    forward_ret(1)
     query_grads(0)
-    forward_ret(1)
     query_grads(1)
 
     for gi in range(GROUPS):
@@ -327,7 +342,7 @@
             else:
                 own_swap(gi).wait_recv()
                 total = own_rx[gi]
-            for j in (3, 1):
+            for j in (3, 1) if gi in TERM_HOPS else (2, 3, 1):
                 for t in range(2):
                     ret_arrived(h, gi, j, t).wait_recv()
                 total = total + ret[h, gi, j].astype(F32)
@@ -347,11 +362,14 @@
         for t in range(2):
             q_swap(gi, t).wait_send()
             kv_swap(gi, t).wait_send()
-            kv_hop(gi, t).wait_send()
-            ex_copy(gi, t).wait_send()
-            for j in (1, 3):
-                for k in range(2):
+            if gi in KV_HOPS:
+                kv_hop(gi, t).wait_send()
+            if gi in TERM_HOPS:
+                ex_copy(gi, t).wait_send()
+            for k in range(2):
+                for j in (1, 3) if gi in KV_HOPS else (1, 2, 3):
                     kv_copy(gi, j, k, t).wait_send()
+                for j in (1, 3) if gi in TERM_HOPS else (1, 2, 3):
                     ret_copy(gi, j, t, k).wait_send()
 
         @pl.when(py == 0)

time: 42.6 us -> 41.4 us (0.972)
  Pallas kernels: 41.8 us -> 40.6 us
    pallas_call x1, Pallas kernels: 39.7 us -> 38.4 us  [shards(): pl.pallas_call(kernel, out_shape=[jax.ShapeDtypeStruct(a.shape, BF16) for...]
where the time goes in v3:
time: 41.4 us; the launch traced here: 41.2 us
  Pallas kernels  40.6 us (98%)
  between operations  0.64 us (2%)
    pallas_call x1, Pallas kernels, shards(): pl.pallas_call(kernel, out_shape=[jax.ShapeDtypeStruct(a.shape, BF16) for...  38.4 us
    pallas_call x1, Pallas kernels, shards(): pl.pallas_call(handed_on, grid=(steps,), out_shape=[jax.ShapeDtypeStruct(...  2.18 us

profile of v3, /device:TPU:1, one launch (start us, length us, event | category | flops | bytes accessed | tf_op | source)
XLA Modules:
  0.0 41.2 jit_solution(12500807922851706984)
XLA Ops:
  0.6 38.4 %shard_map.76 = (bf16[128,4096]{1,0:T(8,128)(2,1)}, bf16[128,512]{1,0:T(8,128)(2,1)}, bf16[128,512]{1,0:T(8,128)(2,1)}) custom-call(s32[4,16]{1,0:T(4,128)} %lengths.1, bf16[128,4096]{1,0:T(8,128)(2,1)} %bitcast.7, bf16[128,512]{1,0:T(8,128)(2,1)} %bitcast.9, bf16[128,512]{1,0:T(8,128)(2,1)} %bitcast.10, bf16[128,4096]{1,0:T(8,128)(2,1)} %bitcast.8), custom_call_target="tpu_custom_call" | custom-call | tf_op jit(solution)/shard_map/pallas_call | solution.py:399
  39.1 2.2 %shard_map.77 = (bf16[128,4096]{1,0:T(8,128)(2,1)}, bf16[128,512]{1,0:T(8,128)(2,1)}, bf16[128,512]{1,0:T(8,128)(2,1)}) custom-call(bf16[128,4096]{1,0:T(8,128)(2,1)} %get-tuple-element.9.dq, bf16[128,512]{1,0:T(8,128)(2,1)} %get-tuple-element.10.dk, bf16[128,512]{1,0:T(8,128)(2,1)} %get-tuple-element.11.dv), custom_call_target="tpu_custom_call" | custom-call | tf_op jit(solution)/shard_map/pallas_call | solution.py:443
